TPU v7x, 32 devices: a whole 2x2x4 slice. The times are simulated.
32 devices in a mesh: groups: 2 (over y), neuron: 4 (over z), row: 2 (over x), sub: 2 (over core).
Axes of the slice: x: 2, y: 2, z: 4, core: 2. Of those that a mesh axis runs over, the one named last changes fastest.
Arguments:
- features: bfloat16 [896, 9216], P(('groups', 'row', 'sub'), 'neuron'), parts along dimension 0, may hold values from -6 to 6
- ln_gain: bfloat16 [9216], P('neuron'), may hold values from 0.099609375 to 1.8984375
- up_weight: bfloat16 [9216, 4608], P(('row', 'sub'), 'neuron'), may hold values from -0.0625 to 0.0625
- up_bias: bfloat16 [4608], P('neuron'), may hold values from -3 to 3
- down_weight: bfloat16 [9216, 4608], P(('row', 'sub'), 'neuron'), may hold values from -0.1875 to 0.1875
- pred_in: bfloat16 [9216, 1024], P(None, 'neuron'), may hold values from -0.0625 to 0.0625
- pred_out: bfloat16 [1024, 36], P('neuron'), may hold values from -0.1875 to 0.1875
- active: int32 [8, 8], P('groups'), parts along dimension 0, may hold values from 0 to 35, as said below
- counts: int32 [8], P('groups'), parts along dimension 0, may hold values from 2 to 8
Outputs:
- mixed: bfloat16 [896, 9216], P(('groups', 'row', 'sub'), 'neuron'), parts along dimension 0
There are 2 independent parts, one for each index of `groups`. A program takes and returns all parts, laid end to end along the dimension named above; an argument that names none is the same for every part. Nothing has to cross between parts.
Inputs may be any that keep to these rules, and one draw needn't show every extreme that they name: `active`: for every row group the entries before its count are distinct block ids, at most 2 of them in any one neuron range of 9 consecutive ids, and every group has a range with exactly 2; entries from its count on are arbitrary block ids.
All inputs are finite; a program needn't handle non-finite values.
Results may differ from a plain program's by a relative error of at most 0.0065.
Values may be sent and summed in bfloat16 or wider, within the bound.
A program may use at most 128 MiB of HBM per device.

v0:
```python
import jax
import jax.numpy as jnp
from jax import lax
from jax.sharding import PartitionSpec as P

BW = 128
CAP = 2


epsilon = 1e-05


def normalize(values, gain, width_all, total, square):
    mean = total / width_all
    spread = square / width_all - mean * mean
    return ((values - mean) * lax.rsqrt(spread + epsilon) * gain.astype(jnp.float32)).astype(
        jnp.bfloat16
    )


def per_device(
    features, ln_gain, up_weight, up_bias, down_weight, pred_in, pred_out, active, counts
):
    group_count = lax.axis_size(("row", "sub"))
    neuron = lax.axis_index("neuron")
    group = lax.axis_index(("row", "sub"))
    slice_rows = up_weight.shape[0]
    blocks = up_weight.shape[1] // BW
    whole, gain_all = (
        lax.all_gather(features, "neuron", axis=1, tiled=True),
        lax.all_gather(ln_gain, "neuron", axis=0, tiled=True),
    )
    values = whole.astype(jnp.float32)
    normed = normalize(
        values,
        gain_all,
        values.shape[1],
        jnp.sum(values, axis=1, keepdims=True),
        jnp.sum(values * values, axis=1, keepdims=True),
    )
    factor = jnp.dot(normed, pred_in, preferred_element_type=jnp.float32).astype(jnp.bfloat16)
    terms = jnp.dot(factor, pred_out, preferred_element_type=jnp.float32)
    scores = lax.psum_scatter(
        terms.astype(jnp.bfloat16), "neuron", scatter_dimension=1, tiled=True
    ).astype(jnp.float32)
    gates = jax.nn.sigmoid(scores)
    live = lax.broadcasted_iota(jnp.int32, active.shape, 1) < counts[:, None]
    local_ids = neuron * blocks + jnp.arange(blocks, dtype=jnp.int32)
    chosen = jnp.any(
        (active[:, :, None] == local_ids[None, None, :]) & live[:, :, None], axis=1
    ).astype(jnp.int32)
    order = jnp.cumsum(chosen, axis=1) - 1
    slots = jnp.arange(CAP, dtype=jnp.int32)
    picks = ((order[:, None, :] == slots[None, :, None]) & (chosen[:, None, :] == 1)).astype(
        jnp.bfloat16
    )
    mine = lax.dynamic_index_in_dim(picks, group, 0, keepdims=False).astype(jnp.float32)
    bias_table = up_bias.reshape(blocks, BW).astype(jnp.float32)
    bias_slots = jnp.sum(mine[:, :, None] * bias_table[None, :, :], axis=1)
    gate_slots = jnp.sum(gates[:, None, :] * mine[None, :, :], axis=2)
    up_local = up_weight.reshape(slice_rows, blocks, BW)
    down_local = down_weight.reshape(slice_rows, blocks, BW)
    paired = jnp.stack((up_local, down_local), 0)
    outgoing = jnp.einsum(
        "gsj,pdjc->gspdc", picks, paired, preferred_element_type=jnp.float32
    ).astype(jnp.bfloat16)
    received = lax.all_to_all(
        outgoing[:, :, :, None], ("row", "sub"), split_axis=0, concat_axis=3, tiled=True
    )
    weights_in = received.reshape(CAP, 2, slice_rows * group_count, BW)
    pre = jnp.einsum("rd,sdc->rsc", normed, weights_in[:, 0], preferred_element_type=jnp.float32)
    hidden = (jax.nn.relu(pre + bias_slots[None]) * gate_slots[:, :, None]).astype(jnp.bfloat16)
    partial_value = jnp.einsum(
        "rsc,sdc->rd", hidden, weights_in[:, 1], preferred_element_type=jnp.float32
    )
    summed = lax.psum_scatter(
        partial_value.astype(jnp.bfloat16), "neuron", scatter_dimension=1, tiled=True
    ).astype(jnp.float32)
    return (features.astype(jnp.float32) + summed).astype(jnp.bfloat16)


def solution(mesh):
    placed = (
        P(("groups", "row", "sub"), "neuron"),
        P("neuron"),
        P(("row", "sub"), "neuron"),
        P("neuron"),
        P(("row", "sub"), "neuron"),
        P(None, "neuron"),
        P("neuron", None),
        P("groups", None),
        P("groups"),
    )
    return jax.shard_map(
        per_device,
        mesh=mesh,
        in_specs=placed,
        out_specs=P(("groups", "row", "sub"), "neuron"),
        check_vma=False,
    )
```

profile of v0, /device:TPU:0, one launch (start us, length us, event | category | flops | bytes accessed | tf_op | source)
XLA Modules:
  0.0 251.7 jit_solution(2653681457146903040)
XLA Ops:
  6.5 0.0 copy-start
  6.5 8.6 %copy.42 = bf16[2304,1152]{0,1:T(8,128)(2,1)} copy(bf16[2304,1152]{1,0:T(8,128)(2,1)} %param.13) | data formatting | bytes 10616832 | tf_op args[4]
  15.1 13.2 %copy.44 = bf16[1,2304,9,128]{3,2,1,0:T(8,128)(2,1)} copy(bf16[1,2304,9,128]{1,3,2,0:T(8,128)(2,1)} %bitcast.67) | data formatting | bytes 10616832 | tf_op jit(solution)/shard_map/stack;reshape | solution.py:63
  28.3 8.6 %copy.41 = bf16[2304,1152]{0,1:T(8,128)(2,1)} copy(bf16[2304,1152]{1,0:T(8,128)(2,1)} %param.11) | data formatting | bytes 10616832 | tf_op args[2]
  36.9 0.0 copy-start.6
  36.9 0.0 copy-start.5
  36.9 13.2 %copy.43 = bf16[1,2304,9,128]{3,2,1,0:T(8,128)(2,1)} copy(bf16[1,2304,9,128]{1,3,2,0:T(8,128)(2,1)} %bitcast.68) | data formatting | bytes 10616832 | tf_op jit(solution)/shard_map/stack;reshape | solution.py:63
  50.0 0.0 copy-done.6
  50.1 0.1 iota_compare_fusion
  50.1 0.0 copy-done.5
  50.1 0.1 and_reduce_fusion
  50.2 0.2 reduce_window_sum.11
  50.4 10.9 %convert_bitcast_fusion = bf16[4,2,2,1,2304,128]{5,0,4,2,1,3:T(4,128)(2,1)} fusion(bf16[1,2304,9,128]{3,2,1,0:T(8,128)(2,1)} %copy.44, bf16[1,2304,9,128]{3,2,1,0:T(8,128)(2,1)} %copy.43, pred[4,2,9,1,1]{2,1,0,4,3:T(4,128)(4,1)S(1)} %fusion.41), kind=kOutput, calls=%fused_computation.6 | convolution fusion | flops 110886912 | bytes 20054088 | tf_op jit(solution)/shard_map/gsj,pdjc->gspdc/dot_general | solution.py:64
  61.4 9.2 %copy.46 = bf16[4,2,2,1,2304,128]{5,4,2,1,3,0:T(8,128)(2,1)} copy(bf16[4,2,2,1,2304,128]{5,0,4,2,1,3:T(4,128)(2,1)} %convert_bitcast_fusion) | data formatting | bytes 18874368 | tf_op jit(solution)/shard_map/broadcast_in_dim | solution.py:68
  70.6 0.0 copy-start.3
  70.6 0.0 copy-start.7
  70.6 0.0 copy-start.4
  70.6 5.9 %all-to-all-start = ((bf16[4,2,2,1,2304,128]{5,4,2,1,3,0:T(8,128)(2,1)}), bf16[4,2,2,1,2304,128]{5,4,2,1,3,0:T(8,128)(2,1)}, u32[]{:S(2)}, u32[]{:S(2)}) async-start(bf16[4,2,2,1,2304,128]{5,4,2,1,3,0:T(8,128)(2,1)} %copy.46), calls=%async_computation | async-start | bytes 18874368 | tf_op jit(solution)/shard_map/all_to_all | solution.py:67
  76.6 0.0 all-gather.3.cloned.1.call-start
  76.6 0.7 all-gather.3.cloned.1.call-update
  77.3 0.0 reduce-scatter.3.cloned.1.call-start
  77.4 0.1 copy.49
  77.5 0.0 copy-done.3
  77.5 14.8 %all-gather = bf16[4,1,2304]{2,1,0:T(2,128)(2,1)S(1)} all-gather(bf16[1,1,2304]{2,1,0:T(2,128)(2,1)S(1)} %reshape.82), channel_id=1, replica_groups=mesh['groups'=2,'neuron'=4,'row'=2,'sub'=2] {'neuron'}, dimensions={0}, use_global_device_ids=true | all-gather | bytes 23040 | tf_op jit(solution)/shard_map/all_gather | solution.py:31
  92.4 0.0 copy-done.7
  92.4 0.6 dynamic-slice
  93.6 0.0 copy-done.4
  93.6 0.1 multiply_reduce_fusion.1
  93.7 33.7 %all-gather.3.cloned.1.call-done = bf16[112,9216]{1,0:T(8,128)(2,1)} async-done(((bf16[112,2304]{1,0:T(8,128)(2,1)}), bf16[112,9216]{1,0:T(8,128)(2,1)}) %all-gather.3.cloned.1.call-update) | async-done | bytes 2064400 | tf_op jit(solution)/shard_map/all_gather | solution.py:30
  127.5 2.2 convert_reduce_fusion
  129.7 0.0 copy-done
  129.7 3.9 %fusion.25 = bf16[112,36]{0,1:T(8,128)(2,1)S(1)} fusion(bf16[256,36]{0,1:T(8,128)(2,1)S(1)} %copy-done, bf16[9216,256]{1,0:T(8,128)(2,1)} %param.14, bf16[112,9216]{1,0:T(8,128)(2,1)} %all-gather.3.cloned.1.call-done, f32[9216]{0:T(1024)S(1)} %bitcast.70, f32[112]{0:T(128)S(1)} %get-tuple-element.8, f32[112]{0:T(128)S(1)} %get-tuple-element.7), kind=kOutput, calls=%fused_computation.24 | convolution fusion | flops 535740352 | bytes 6847232 | tf_op jit(solution)/shard_map/dot_general | solution.py:42
  133.6 0.1 copy.50
  133.8 16.9 %all-reduce = bf16[112,36]{1,0:T(8,128)(2,1)S(1)} all-reduce(bf16[112,36]{1,0:T(8,128)(2,1)S(1)} %copy.50), channel_id=2, replica_groups=mesh['groups'=2,'neuron'=4,'row'=2,'sub'=2] {'neuron'}, use_global_device_ids=true, to_apply=%region_5.6.clone | all-reduce | flops 4032 | bytes 16128
  150.7 0.1 constant_dynamic-slice_fusion
  150.7 0.1 copy.51
  150.9 0.1 multiply_reduce_fusion
  150.9 0.0 copy-start.1
  151.0 30.7 %all-to-all-done = bf16[4,2,2,1,2304,128]{5,4,2,1,3,0:T(8,128)(2,1)} async-done(((bf16[4,2,2,1,2304,128]{5,4,2,1,3,0:T(8,128)(2,1)}), bf16[4,2,2,1,2304,128]{5,4,2,1,3,0:T(8,128)(2,1)}, u32[]{:S(2)}, u32[]{:S(2)}) %all-to-all-start) | async-done | bytes 9437216 | tf_op jit(solution)/shard_map/all_to_all | solution.py:67
  181.6 8.2 %copy.47 = bf16[4,2,2,1,2304,128]{5,4,0,2,1,3:T(8,128)(2,1)} copy(bf16[4,2,2,1,2304,128]{5,4,2,1,3,0:T(8,128)(2,1)} %all-to-all-done) | data formatting | bytes 18874368 | tf_op jit(solution)/shard_map/all_to_all | solution.py:67
  189.9 0.0 copy-done.1
  189.9 0.0 copy-start.2
  189.9 8.6 %fusion.3 = bf16[112,9216]{1,0:T(8,128)(2,1)} fusion(bf16[2,2,9216,128]{3,2,1,0:T(8,128)(2,1)} %bitcast.69, f32[112,2]{0,1:T(2,128)S(1)} %multiply_reduce_fusion, f32[2,128]{1,0:T(2,128)S(1)} %multiply_reduce_fusion.1, bf16[112,9216]{1,0:T(8,128)(2,1)S(1)} %copy-done.1, f32[9216]{0:T(1024)S(1)} %bitcast.71, f32[112]{0:T(128)S(1)} %get-tuple-element.8, ...), kind=kOutput, calls=%fused_computation.5 | convolution fusion | flops 1063272448 | bytes 13605632 | tf_op jit(solution)/shard_map/rsc,sdc->rd/dot_general | solution.py:73
  198.5 0.0 reduce-scatter.3.cloned.1.call-update
  198.5 44.4 %reduce-scatter.3.cloned.1.call-done = bf16[112,2304]{1,0:T(8,128)(2,1)} async-done(((bf16[112,9216]{1,0:T(8,128)(2,1)}), bf16[112,2304]{1,0:T(8,128)(2,1)}) %reduce-scatter.3.cloned.1.call-update) | async-done | bytes 516112 | tf_op jit(solution)/shard_map/reduce_scatter | solution.py:76
  242.9 0.0 copy-done.2
  242.9 2.0 add_convert_fusion
  (11 shorter events, 0.1 us)
Async XLA Ops:
  6.5 123.2 %copy-start = (bf16[256,36]{0,1:T(8,128)(2,1)S(1)}, bf16[256,36]{0,1:T(8,128)(2,1)}, u32[]{:S(2)}) copy-start(bf16[256,36]{0,1:T(8,128)(2,1)} %param.15) | copy-start | bytes 55300
  36.9 13.2 %copy-start.6 = (s32[4]{0:T(128)S(1)}, s32[4]{0:T(128)}, u32[]{:S(2)}) copy-start(s32[4]{0:T(128)} %param.17) | copy-start | bytes 52
  36.9 13.3 %copy-start.5 = (s32[4,8]{1,0:T(4,128)S(1)}, s32[4,8]{1,0:T(4,128)}, u32[]{:S(2)}) copy-start(s32[4,8]{1,0:T(4,128)} %param.16) | copy-start | bytes 388
  70.6 6.9 %copy-start.3 = (bf16[2304]{0:T(1024)(128)(2,1)S(1)}, bf16[2304]{0:T(1024)(128)(2,1)}, u32[]{:S(2)}) copy-start(bf16[2304]{0:T(1024)(128)(2,1)} %param.10) | copy-start | bytes 13828
  70.6 21.8 %copy-start.7 = (u32[32]{0:T(128)S(1)}, u32[32]{0:T(128)}, u32[]{:S(2)}) copy-start(u32[32]{0:T(128)} %constant.45) | copy-start | bytes 388
  70.6 23.0 %copy-start.4 = (bf16[1152]{0:T(1024)(128)(2,1)S(1)}, bf16[1152]{0:T(1024)(128)(2,1)}, u32[]{:S(2)}) copy-start(bf16[1152]{0:T(1024)(128)(2,1)} %param.12) | copy-start | bytes 6916
  70.6 111.0 %all-to-all-start = ((bf16[4,2,2,1,2304,128]{5,4,2,1,3,0:T(8,128)(2,1)}), bf16[4,2,2,1,2304,128]{5,4,2,1,3,0:T(8,128)(2,1)}, u32[]{:S(2)}, u32[]{:S(2)}) async-start(bf16[4,2,2,1,2304,128]{5,4,2,1,3,0:T(8,128)(2,1)} %copy.46), calls=%async_computation | async-start | bytes 18874368 | tf_op jit(solution)/shard_map/all_to_all | solution.py:67
  76.6 50.9 %all-gather.3.cloned.1.call-start = ((), (), s32[]{:S(2)}) async-start(), calls=%async_computation.2 | async-start | bytes 2580480 | tf_op jit(solution)/shard_map/all_gather | solution.py:30
  77.3 165.6 %reduce-scatter.3.cloned.1.call-start = ((), (), s32[]{:S(2)}) async-start(), calls=%async_computation.3 | async-start | bytes 2580480 | tf_op jit(solution)/shard_map/reduce_scatter | solution.py:76
  150.9 38.9 %copy-start.1 = (bf16[112,9216]{1,0:T(8,128)(2,1)S(1)}, bf16[112,9216]{1,0:T(8,128)(2,1)}, u32[]{:S(2)}) copy-start(bf16[112,9216]{1,0:T(8,128)(2,1)} %all-gather.3.cloned.1.call-done) | copy-start | bytes 6193156
  189.9 53.1 %copy-start.2 = (bf16[112,2304]{1,0:T(8,128)(2,1)S(1)}, bf16[112,2304]{1,0:T(8,128)(2,1)}, u32[]{:S(2)}) copy-start(bf16[112,2304]{1,0:T(8,128)(2,1)} %param.9) | copy-start | bytes 1548292
Sparse Core Ops, SparseCore 0:
  79.0 48.4 all-gather.2
  198.6 44.2 reduce-scatter.2
where the time goes:
time: 253 us; the launch traced here: 252 us
  waiting for transfers between devices  110 us (43%)
  local copies, waits for them, and re-layouts  62 us (25%)
  blocking collectives  31.7 us (13%)
  matrix products  23.5 us (9%)
  between operations  14.2 us (6%)
  starting transfers between devices  6.02 us (2%)
  other arithmetic  4.85 us (2%)
    reduce_scatter x1, waiting for transfers between devices, per_device(): lax.psum_scatter(partial_value.astype(jnp.bfloat16), 'neuron', scatter_di...  44.4 us
    all_gather x1, waiting for transfers between devices, per_device(): lax.all_gather(features, 'neuron', axis=1, tiled=True)  33.7 us
    all_to_all x1, waiting for transfers between devices, per_device(): lax.all_to_all(outgoing[:, :, :, None], ('row', 'sub'), split_axis=0, con...  30.7 us
    another operation x2, local copies, waits for them, and re-layouts, per_device(): paired = jnp.stack((up_local, down_local), 0)  26.4 us
    unnamed x21, local copies, waits for them, and re-layouts  17.8 us
    unnamed x1, blocking collectives  16.9 us
    all_gather x1, blocking collectives, per_device(): lax.all_gather(ln_gain, 'neuron', axis=0, tiled=True)  14.8 us
    dot_general x1, matrix products, per_device(): jnp.einsum('gsj,pdjc->gspdc', picks, paired, preferred_element_type=jnp.f...  10.9 us
  transfers between devices with their start and end apart: 3, of which 3 were waited for; matrix products, arithmetic and copies ran while one was open for 3% of the time, Pallas kernels for 0%

commit v1 on v0

--- a/solution.py
+++ b/solution.py
@@ -1,6 +1,8 @@
 import jax
 import jax.numpy as jnp
 from jax import lax
+from jax.experimental import pallas as pl
+from jax.experimental.pallas import tpu as pltpu
 from jax.sharding import PartitionSpec as P
 
 BW = 128
@@ -78,6 +80,286 @@
     ).astype(jnp.float32)
     return (features.astype(jnp.float32) + summed).astype(jnp.bfloat16)
 
+N = 4
+PARTS = ((0, 64), (64, 48))
+MESH = pl.DeviceIdType.MESH
+
+
+def layer_kernel(
+    ids, x_ref, gain_ref, bias_ref, pick_ref, pout_ref, up_hbm, down_hbm, pin_hbm, out_ref,
+    zbuf, zgain, xin, stats, terms, term_out, pre_out, pre_in, hid, outp, pbuf, rbuf,
+    up_v, down_v, pin_v,
+    z_ss, z_rs, g_ss, g_rs, x_ss, x_rs, s_ss, s_rs, t_ss, t_rs, p_ss, p_rs, h_ss, h_rs,
+    o_ss, o_rs, r_ss, r_rs, w_sem,
+):
+    n = lax.axis_index("neuron")
+    g = lax.axis_index("row") * 2 + lax.axis_index("sub")
+    slice_w = x_ref.shape[1]
+    full = slice_w * N
+    f32, bf16 = jnp.float32, jnp.bfloat16
+
+    def zdev(m):
+        return {"neuron": m}
+
+    def pdev(w):
+        return {"row": w // 2, "sub": lax.rem(w, 2)}
+
+    def send(src, dst, ss, rs, dev):
+        return pltpu.make_async_remote_copy(
+            src_ref=src, dst_ref=dst, send_sem=ss, recv_sem=rs, device_id=dev, device_id_type=MESH
+        )
+
+    blocks = up_v.shape[0]
+    loads = [[pltpu.make_async_copy(pin_hbm, pin_v, w_sem.at[0, 0])]]
+    for i, (a, b) in enumerate(((up_hbm, up_v), (down_hbm, down_v))):
+        loads.append(
+            [
+                pltpu.make_async_copy(a.at[:, pl.ds(j * BW, BW)], b.at[j], w_sem.at[1 + i, j])
+                for j in range(blocks)
+            ]
+        )
+    for group in loads:
+        for load in group:
+            load.start()
+    zpeer = [lax.rem(n + k, N) for k in range(N)]
+    ppeer = [lax.rem(g + k, N) for k in range(N)]
+    barrier = pltpu.get_barrier_semaphore()
+    for k in range(1, N):
+        pl.semaphore_signal(barrier, inc=1, device_id=zdev(zpeer[k]), device_id_type=MESH)
+        pl.semaphore_signal(barrier, inc=1, device_id=pdev(ppeer[k]), device_id_type=MESH)
+    pl.semaphore_wait(barrier, 2 * (N - 1))
+
+    sent = []
+
+    def go(copy):
+        copy.start()
+        sent.append(copy)
+
+    def rows(c):
+        return pl.ds(PARTS[c][0], PARTS[c][1])
+
+    chunks = range(len(PARTS))
+    for c in chunks:
+        for k in range(1, N):
+            go(send(x_ref.at[rows(c)], zbuf.at[n, rows(c)], z_ss.at[k, c], z_rs.at[n, c], zdev(zpeer[k])))
+            if c == 0:
+                go(send(gain_ref, zgain.at[n], g_ss.at[k], g_rs.at[n], zdev(zpeer[k])))
+    zbuf[n] = x_ref[...]
+    zgain[n] = gain_ref[...]
+
+    for c in chunks:
+        for k in (1, 2, 3, 0):
+            w = ppeer[k]
+
+            @pl.when(w != n)
+            def _(w=w, c=c):
+                send(x_ref.at[rows(c)], zbuf.at[w, rows(c)], z_ss.at[1, c], z_rs.at[w, c], zdev(zpeer[1])).wait_recv()
+
+            if k:
+                go(send(zbuf.at[w, rows(c)], xin.at[g, rows(c)], x_ss.at[k, c], x_rs.at[g, c], pdev(w)))
+    for k in range(1, N):
+        m = zpeer[k]
+        send(gain_ref, zgain.at[m], g_ss.at[1], g_rs.at[m], zdev(m)).wait_recv()
+
+    def add_stats(m, carry):
+        total, square = carry
+        v = zbuf[m].astype(f32)
+        return (
+            total + jnp.sum(v, axis=1, keepdims=True),
+            square + jnp.sum(v * v, axis=1, keepdims=True),
+        )
+
+    zero = jnp.zeros((x_ref.shape[0], 1), f32)
+    total, square = lax.fori_loop(0, N, add_stats, (zero, zero))
+    mean = total / full
+    scale = lax.rsqrt(square / full - mean * mean + epsilon)
+    lane = lax.broadcasted_iota(jnp.int32, (x_ref.shape[0], 128), 1)
+    stats[g] = jnp.where(lane < 64, mean, scale)
+    for k in range(1, N):
+        go(send(stats.at[g], stats.at[g], s_ss.at[k], s_rs.at[g], pdev(ppeer[k])))
+
+    def norm(values, mu, sc, gain):
+        return ((values.astype(f32) - mu) * sc * gain).astype(bf16)
+
+    for load in loads[0]:
+        load.wait()
+
+    def add_factor(m, acc):
+        block = pin_v[pl.ds(pl.multiple_of(m * slice_w, 128), slice_w), :]
+        return acc + jnp.dot(norm(zbuf[m], mean, scale, zgain[m]), block, preferred_element_type=f32)
+
+    factor = lax.fori_loop(0, N, add_factor, jnp.zeros((x_ref.shape[0], pin_v.shape[1]), f32))
+    term_out[...] = jnp.dot(factor.astype(bf16), pout_ref[...], preferred_element_type=f32).astype(bf16)
+    terms[n] = term_out[...]
+    for k in range(1, N):
+        go(send(term_out, terms.at[n], t_ss.at[k], t_rs.at[n], zdev(zpeer[k])))
+
+    def picked(ref, q):
+        return jnp.concatenate((ref[ids[2 * q]], ref[ids[2 * q + 1]]), axis=1)
+
+    for load in loads[1]:
+        load.wait()
+    xin[g] = zbuf[g]
+
+    def up(k, _):
+        q = lax.rem(g + k, N)
+
+        @pl.when(k < N)
+        def _():
+            for c in chunks:
+                send(x_ref.at[rows(c)], xin.at[q, rows(c)], x_ss.at[1, c], x_rs.at[q, c], pdev(q)).wait_recv()
+            send(stats.at[g], stats.at[q], s_ss.at[1], s_rs.at[q], pdev(q)).wait_recv()
+
+        st = stats[q]
+        normed = norm(xin[q], st[:, 0:1], st[:, 64:65], zgain[g])
+        pre = jnp.dot(normed, picked(up_v, q), preferred_element_type=f32)
+        pre_out[q] = pre.astype(bf16)
+
+        @pl.when(k < N)
+        def _():
+            send(pre_out.at[q], pre_in.at[g], p_ss.at[lax.rem(k, N)], p_rs.at[g], pdev(q)).start()
+
+        return 0
+
+    lax.fori_loop(1, N + 1, up, 0)
+    for k in range(1, N):
+        sent.append(send(pre_out.at[ppeer[k]], pre_in.at[g], p_ss.at[k], p_rs.at[g], pdev(ppeer[k])))
+
+    for k in range(1, N):
+        m = zpeer[k]
+        send(term_out, terms.at[m], t_ss.at[1], t_rs.at[m], zdev(m)).wait_recv()
+    scores = jnp.zeros((x_ref.shape[0], 128), f32)
+    for m in range(N):
+        scores = scores + terms[m].astype(f32)
+    gates = jax.nn.sigmoid(scores)
+    gate = [jnp.sum(gates * pick_ref[j], axis=1, keepdims=True) for j in range(CAP)]
+    pre = pre_out[g].astype(f32)
+    for k in range(1, N):
+        q = ppeer[k]
+        send(pre_out.at[g], pre_in.at[q], p_ss.at[1], p_rs.at[q], pdev(q)).wait_recv()
+        pre = pre + pre_in[q].astype(f32)
+    hidden = [
+        (jnp.maximum(pre[:, j * BW : (j + 1) * BW] + bias_ref[j], 0.0) * gate[j]).astype(bf16)
+        for j in range(2)
+    ]
+    hid[g] = jnp.concatenate(hidden, axis=1)
+    for k in range(1, N):
+        go(send(hid.at[g], hid.at[g], h_ss.at[k], h_rs.at[g], pdev(ppeer[k])))
+
+    for load in loads[2]:
+        load.wait()
+
+    def down(k, _):
+        q = lax.rem(g + k, N)
+
+        @pl.when(k < N)
+        def _():
+            send(hid.at[g], hid.at[q], h_ss.at[1], h_rs.at[q], pdev(q)).wait_recv()
+
+        outp[q] = lax.dot_general(
+            hid[q], picked(down_v, q), (((1,), (1,)), ((), ())), preferred_element_type=f32
+        ).astype(bf16)
+
+        @pl.when(k < N)
+        def _():
+            for c in chunks:
+                send(outp.at[q, rows(c)], pbuf.at[g, rows(c)], o_ss.at[lax.rem(k, N), c], o_rs.at[g, c], pdev(q)).start()
+
+        return 0
+
+    lax.fori_loop(1, N + 1, down, 0)
+    for k in range(1, N):
+        for c in chunks:
+            sent.append(send(outp.at[ppeer[k], rows(c)], pbuf.at[g, rows(c)], o_ss.at[k, c], o_rs.at[g, c], pdev(ppeer[k])))
+    pbuf[g] = outp[g]
+    for c in chunks:
+        for k in (1, 2, 3, 0):
+            m = zpeer[k]
+
+            @pl.when(m != g)
+            def _(m=m, c=c):
+                send(outp.at[0, rows(c)], pbuf.at[m, rows(c)], o_ss.at[1, c], o_rs.at[m, c], pdev(ppeer[1])).wait_recv()
+
+            if k:
+                go(send(pbuf.at[m, rows(c)], rbuf.at[n, rows(c)], r_ss.at[k, c], r_rs.at[n, c], zdev(m)))
+    for c in chunks:
+        acc = pbuf[n, rows(c)].astype(f32)
+        for k in range(1, N):
+            m = zpeer[k]
+            send(pbuf.at[m, rows(c)], rbuf.at[m, rows(c)], r_ss.at[1, c], r_rs.at[m, c], zdev(m)).wait_recv()
+            acc = acc + rbuf[m, rows(c)].astype(f32)
+        out_ref[rows(c)] = (x_ref[rows(c)].astype(f32) + acc).astype(bf16)
+    for copy in sent:
+        copy.wait_send()
+
+
+def fused_device(
+    features, ln_gain, up_weight, up_bias, down_weight, pred_in, pred_out, active, counts
+):
+    neuron = lax.axis_index("neuron")
+    blocks = up_weight.shape[1] // BW
+    height, slice_w = features.shape
+    live = lax.broadcasted_iota(jnp.int32, active.shape, 1) < counts[:, None]
+    local_ids = neuron * blocks + jnp.arange(blocks, dtype=jnp.int32)
+    chosen = jnp.any((active[:, :, None] == local_ids[None, None, :]) & live[:, :, None], axis=1)
+    number = jnp.arange(blocks, dtype=jnp.int32)[None, :]
+    lowest = jnp.min(jnp.where(chosen, number, blocks), axis=1)
+    highest = jnp.max(jnp.where(chosen, number, -1), axis=1)
+    places = jnp.stack((jnp.minimum(lowest, blocks - 1), jnp.maximum(highest, 0)), axis=1)
+    group = lax.axis_index(("row", "sub"))
+    mine = lax.dynamic_index_in_dim(places, group, 0, keepdims=False)
+    low = lax.dynamic_index_in_dim(lowest, group, 0, keepdims=False)
+    high = lax.dynamic_index_in_dim(highest, group, 0, keepdims=False)
+    valid = jnp.stack((high >= 0, high > low))
+    lanes = jnp.arange(128, dtype=jnp.int32)[None, :]
+    pick = ((lanes == neuron * blocks + mine[:, None]) & valid[:, None]).astype(jnp.float32)[:, None]
+    hot = (number == mine[:, None]).astype(jnp.float32)
+    bias_table = up_bias.reshape(blocks, BW).astype(jnp.float32)
+    bias = jnp.sum(hot[:, :, None] * bias_table[None], axis=1)[:, None]
+    gain = ln_gain.astype(jnp.float32).reshape(1, slice_w)
+    pout = jnp.pad(pred_out, ((0, 0), (0, 128 - pred_out.shape[1])))
+    vmem = pl.BlockSpec(memory_space=pltpu.VMEM)
+    hbm = pl.BlockSpec(memory_space=pl.ANY)
+    nc = len(PARTS)
+    bf16, f32 = jnp.bfloat16, jnp.float32
+    dma = pltpu.SemaphoreType.DMA
+    return pl.pallas_call(
+        layer_kernel,
+        out_shape=jax.ShapeDtypeStruct(features.shape, bf16),
+        in_specs=[pl.BlockSpec(memory_space=pltpu.SMEM)] + [vmem] * 5 + [hbm] * 3,
+        out_specs=vmem,
+        scratch_shapes=[
+            pltpu.VMEM((N, height, slice_w), bf16),
+            pltpu.VMEM((N, 1, slice_w), f32),
+            pltpu.VMEM((N, height, slice_w), bf16),
+            pltpu.VMEM((N, height, 128), f32),
+            pltpu.VMEM((N, height, 128), bf16),
+            pltpu.VMEM((height, 128), bf16),
+            pltpu.VMEM((N, height, CAP * BW), bf16),
+            pltpu.VMEM((N, height, CAP * BW), bf16),
+            pltpu.VMEM((N, height, CAP * BW), bf16),
+            pltpu.VMEM((N, height, slice_w), bf16),
+            pltpu.VMEM((N, height, slice_w), bf16),
+            pltpu.VMEM((N, height, slice_w), bf16),
+            pltpu.VMEM((blocks, up_weight.shape[0], BW), bf16),
+            pltpu.VMEM((blocks, down_weight.shape[0], BW), bf16),
+            pltpu.VMEM(pred_in.shape, bf16),
+            dma((N, nc)), dma((N, nc)),
+            dma((N,)), dma((N,)),
+            dma((N, nc)), dma((N, nc)),
+            dma((N,)), dma((N,)),
+            dma((N,)), dma((N,)),
+            dma((N,)), dma((N,)),
+            dma((N,)), dma((N,)),
+            dma((N, nc)), dma((N, nc)),
+            dma((N, nc)), dma((N, nc)),
+            dma((3, blocks)),
+        ],
+        compiler_params=pltpu.CompilerParams(
+            collective_id=0, has_side_effects=True, vmem_limit_bytes=50 * 1024 * 1024
+        ),
+    )(places.reshape(-1), features, gain, bias, pick, pout, up_weight, down_weight, pred_in)
+
 
 def solution(mesh):
     placed = (
@@ -91,8 +373,9 @@
         P("groups", None),
         P("groups"),
     )
+    small = mesh.shape["neuron"] == N and mesh.shape["row"] == 2 and mesh.shape["sub"] == 2
     return jax.shard_map(
-        per_device,
+        fused_device if small else per_device,
         mesh=mesh,
         in_specs=placed,
         out_specs=P(("groups", "row", "sub"), "neuron"),

time: 253 us -> 134 us (0.53)
  the two profiles are of different devices: /device:TPU:0 before, /device:TPU:25 now
where the time goes in v1:
time: 134 us
  Pallas kernels  124 us (93%)
  local copies, waits for them, and re-layouts  5.02 us (4%)
  other arithmetic  2.61 us (2%)
  between operations  2.03 us (2%)
    pallas_call x1, Pallas kernels, fused_device(): pl.pallas_call(layer_kernel, out_shape=jax.ShapeDtypeStruct(features.shap...  124 us
    unnamed x4, local copies, waits for them, and re-layouts  2.68 us

profile of v1, /device:TPU:25, one launch (start us, length us, event | category | flops | bytes accessed | tf_op | source)
XLA Modules:
  0.0 133.6 jit_solution(11646370008171857856)
XLA Ops:
  0.0 0.7 iota_compare_fusion.1
  0.7 0.8 and_reduce_fusion
  1.5 0.2 select_reduce_fusion.1
  1.7 0.6 dynamic_slice.12
  2.9 0.7 dynamic_slice.13
  4.9 0.1 pad_add_fusion
  5.0 0.2 dynamic-slice_reduce_fusion
  5.2 0.1 and_convert_fusion.pick_ref
  5.3 0.1 copy.14
  5.4 0.1 reshape.147.ids
  5.5 0.7 bitcast_convert_fusion
  6.2 0.1 multiply_reduce_fusion
  6.2 0.7 reshape.151.gain_ref
  6.9 0.9 copy.15
  7.8 0.0 copy-start
  7.8 1.0 copy-done
  8.9 124.0 %shard_map.91 = bf16[112,2304]{1,0:T(8,128)(2,1)S(1)} custom-call(s32[8]{0:T(128)S(1)} %reshape.147.ids, bf16[112,2304]{1,0:T(8,128)(2,1)S(1)} %copy-done, f32[1,2304]{1,0:T(1,128)S(1)} %reshape.151.gain_ref, f32[2,1,128]{2,1,0:T(1,128)S(1)} %bitcast.8, f32[2,1,128]{2,1,0:T(1,128)S(1)} %and_convert_fusion.pick_ref, bf16[256,128]{1,0:T(8,128)(2,1)S(1)} %pad.4.pout_ref, ...), custom_call_target="tpu_custom_call" | custom-call | tf_op jit(solution)/shard_map/pallas_call | solution.py:326
  132.8 0.8 copy.17
  (6 shorter events, 0.0 us)
Async XLA Ops:
  7.8 1.0 copy-start

commit v2 on v1

--- a/solution.py
+++ b/solution.py
@@ -81,19 +81,20 @@
     return (features.astype(jnp.float32) + summed).astype(jnp.bfloat16)
 
 N = 4
-PARTS = ((0, 64), (64, 48))
+PARTS = ((0, 32), (32, 32), (64, 32), (96, 16))
 MESH = pl.DeviceIdType.MESH
 
 
 def layer_kernel(
     ids, x_ref, gain_ref, bias_ref, pick_ref, pout_ref, up_hbm, down_hbm, pin_hbm, out_ref,
-    zbuf, zgain, xin, stats, terms, term_out, pre_out, pre_in, hid, outp, pbuf, rbuf,
+    zbuf, zgain, xin, stats, terms, term_out, pre_out, pre_in, hid, outp, pbuf, rup, rdn,
     up_v, down_v, pin_v,
     z_ss, z_rs, g_ss, g_rs, x_ss, x_rs, s_ss, s_rs, t_ss, t_rs, p_ss, p_rs, h_ss, h_rs,
-    o_ss, o_rs, r_ss, r_rs, w_sem,
+    o_ss, o_rs, u_ss, u_rs, d_ss, d_rs, w_sem,
 ):
     n = lax.axis_index("neuron")
-    g = lax.axis_index("row") * 2 + lax.axis_index("sub")
+    row, sub = lax.axis_index("row"), lax.axis_index("sub")
+    g = row * 2 + sub
     slice_w = x_ref.shape[1]
     full = slice_w * N
     f32, bf16 = jnp.float32, jnp.bfloat16
@@ -122,7 +123,12 @@
         for load in group:
             load.start()
     zpeer = [lax.rem(n + k, N) for k in range(N)]
-    ppeer = [lax.rem(g + k, N) for k in range(N)]
+
+    def plane(k):
+        flip_row, flip_sub = 1 - k // 3, lax.rem(k // 2, 2)
+        return 2 * (row + flip_row - 2 * row * flip_row) + sub + flip_sub - 2 * sub * flip_sub
+
+    ppeer = [g] + [plane(jnp.int32(k)) for k in range(1, N)]
     barrier = pltpu.get_barrier_semaphore()
     for k in range(1, N):
         pl.semaphore_signal(barrier, inc=1, device_id=zdev(zpeer[k]), device_id_type=MESH)
@@ -139,24 +145,39 @@
         return pl.ds(PARTS[c][0], PARTS[c][1])
 
     chunks = range(len(PARTS))
-    for c in chunks:
-        for k in range(1, N):
-            go(send(x_ref.at[rows(c)], zbuf.at[n, rows(c)], z_ss.at[k, c], z_rs.at[n, c], zdev(zpeer[k])))
-            if c == 0:
-                go(send(gain_ref, zgain.at[n], g_ss.at[k], g_rs.at[n], zdev(zpeer[k])))
+    def hop(m, c, up, src):
+        return send(
+            src, zbuf.at[m, rows(c)], z_ss.at[m, c, 0 if up else 1], z_rs.at[m, c], zdev(n + 1 if up else n - 1)
+        )
+
+    def guarded(cond, fn):
+        pl.when(cond)(fn)
+
+    for c in chunks:
+        guarded(n < N - 1, lambda c=c: hop(n, c, True, x_ref.at[rows(c)]).start())
+        guarded(n > 0, lambda c=c: hop(n, c, False, x_ref.at[rows(c)]).start())
+    for k in range(1, N):
+        go(send(gain_ref, zgain.at[n], g_ss.at[k], g_rs.at[n], zdev(zpeer[k])))
     zbuf[n] = x_ref[...]
     zgain[n] = gain_ref[...]
 
-    for c in chunks:
-        for k in (1, 2, 3, 0):
-            w = ppeer[k]
-
-            @pl.when(w != n)
-            def _(w=w, c=c):
-                send(x_ref.at[rows(c)], zbuf.at[w, rows(c)], z_ss.at[1, c], z_rs.at[w, c], zdev(zpeer[1])).wait_recv()
-
-            if k:
-                go(send(zbuf.at[w, rows(c)], xin.at[g, rows(c)], x_ss.at[k, c], x_rs.at[g, c], pdev(w)))
+    def inward(m, c, src):
+        return send(src, xin.at[g, rows(c)], x_ss.at[m, c], x_rs.at[g, c], pdev(m))
+
+    for c in chunks:
+        guarded(n != g, lambda c=c: inward(n, c, x_ref.at[rows(c)]).start())
+    for far in range(1, N):
+        for c in chunks:
+            for up in (True, False):
+                m = n - far if up else n + far
+
+                def arrive(m=m, c=c, up=up):
+                    block = zbuf.at[m, rows(c)]
+                    send(x_ref.at[rows(c)], block, z_ss.at[m, c, 0], z_rs.at[m, c], zdev(zpeer[1])).wait_recv()
+                    guarded(n < N - 1 if up else n > 0, lambda: hop(m, c, up, block).start())
+                    guarded(m != g, lambda: inward(m, c, block).start())
+
+                guarded(m >= 0 if up else m < N, arrive)
     for k in range(1, N):
         m = zpeer[k]
         send(gain_ref, zgain.at[m], g_ss.at[1], g_rs.at[m], zdev(m)).wait_recv()
@@ -202,7 +223,7 @@
     xin[g] = zbuf[g]
 
     def up(k, _):
-        q = lax.rem(g + k, N)
+        q = plane(k)
 
         @pl.when(k < N)
         def _():
@@ -250,7 +271,7 @@
         load.wait()
 
     def down(k, _):
-        q = lax.rem(g + k, N)
+        q = plane(k)
 
         @pl.when(k < N)
         def _():
@@ -259,36 +280,81 @@
         outp[q] = lax.dot_general(
             hid[q], picked(down_v, q), (((1,), (1,)), ((), ())), preferred_element_type=f32
         ).astype(bf16)
-
-        @pl.when(k < N)
-        def _():
-            for c in chunks:
-                send(outp.at[q, rows(c)], pbuf.at[g, rows(c)], o_ss.at[lax.rem(k, N), c], o_rs.at[g, c], pdev(q)).start()
-
         return 0
 
-    lax.fori_loop(1, N + 1, down, 0)
-    for k in range(1, N):
-        for c in chunks:
-            sent.append(send(outp.at[ppeer[k], rows(c)], pbuf.at[g, rows(c)], o_ss.at[k, c], o_rs.at[g, c], pdev(ppeer[k])))
+    def outward(k, c):
+        q = ppeer[k]
+        return send(outp.at[q, rows(c)], pbuf.at[g, rows(c)], o_ss.at[k, c], o_rs.at[g, c], pdev(q))
+
+    lax.fori_loop(1, 3, down, 0)
+    for c in chunks:
+        for k in (1, 2):
+            go(outward(k, c))
+    lax.fori_loop(3, N + 1, down, 0)
+    for c in chunks:
+        go(outward(3, c))
     pbuf[g] = outp[g]
-    for c in chunks:
-        for k in (1, 2, 3, 0):
-            m = zpeer[k]
-
-            @pl.when(m != g)
-            def _(m=m, c=c):
-                send(outp.at[0, rows(c)], pbuf.at[m, rows(c)], o_ss.at[1, c], o_rs.at[m, c], pdev(ppeer[1])).wait_recv()
-
-            if k:
-                go(send(pbuf.at[m, rows(c)], rbuf.at[n, rows(c)], r_ss.at[k, c], r_rs.at[n, c], zdev(m)))
-    for c in chunks:
-        acc = pbuf[n, rows(c)].astype(f32)
-        for k in range(1, N):
-            m = zpeer[k]
-            send(pbuf.at[m, rows(c)], rbuf.at[m, rows(c)], r_ss.at[1, c], r_rs.at[m, c], zdev(m)).wait_recv()
-            acc = acc + rbuf[m, rows(c)].astype(f32)
-        out_ref[rows(c)] = (x_ref[rows(c)].astype(f32) + acc).astype(bf16)
+
+    def rise(m, c, up):
+        at = pbuf.at[m, rows(c)]
+        if up:
+            return send(at, rup.at[m, rows(c)], u_ss.at[m, c], u_rs.at[m, c], zdev(n + 1))
+        return send(at, rdn.at[m, rows(c)], d_ss.at[m, c], d_rs.at[m, c], zdev(n - 1))
+
+    def landed(m, c, up):
+        buf, sems = (rup, u_rs) if up else (rdn, d_rs)
+        send(x_ref.at[rows(c)], buf.at[m, rows(c)], u_ss.at[m, c], sems.at[m, c], zdev(zpeer[1])).wait_recv()
+
+    def own(m, c):
+        def wait():
+            send(outp.at[0, rows(c)], pbuf.at[m, rows(c)], o_ss.at[1, c], o_rs.at[m, c], pdev(ppeer[1])).wait_recv()
+
+        guarded(m != g, wait)
+
+    for c in chunks:
+        for far in (3, 2, 1):
+            for up in (True, False):
+                m = n + far if up else n - far
+
+                def forward(m=m, c=c, up=up):
+                    own(m, c)
+
+                    def add():
+                        landed(m, c, up)
+                        other = rup if up else rdn
+                        pbuf[m, rows(c)] = (
+                            pbuf[m, rows(c)].astype(f32) + other[m, rows(c)].astype(f32)
+                        ).astype(bf16)
+
+                    guarded(n > 0 if up else n < N - 1, add)
+                    rise(m, c, up).start()
+
+                guarded(m < N if up else m >= 0, forward)
+    for c in chunks:
+        own(n, c)
+
+        def middle(c=c):
+            landed(n, c, True)
+            landed(n, c, False)
+            total = rup[n, rows(c)].astype(f32) + rdn[n, rows(c)].astype(f32) + pbuf[n, rows(c)].astype(f32)
+            out_ref[rows(c)] = (x_ref[rows(c)].astype(f32) + total).astype(bf16)
+
+        def edge(c=c, up=True):
+            landed(n, c, up)
+            other = rup if up else rdn
+            total = other[n, rows(c)].astype(f32) + pbuf[n, rows(c)].astype(f32)
+            out_ref[rows(c)] = (x_ref[rows(c)].astype(f32) + total).astype(bf16)
+
+        guarded(n == 0, lambda c=c: edge(c, False))
+        guarded(n == N - 1, lambda c=c: edge(c, True))
+        guarded((n > 0) & (n < N - 1), middle)
+    for c in chunks:
+        for m in range(N):
+            guarded((n >= m) & (n < N - 1), lambda m=m, c=c: hop(m, c, True, x_ref.at[rows(c)]).wait_send())
+            guarded((n <= m) & (n > 0), lambda m=m, c=c: hop(m, c, False, x_ref.at[rows(c)]).wait_send())
+            guarded(g != m, lambda m=m, c=c: inward(m, c, x_ref.at[rows(c)]).wait_send())
+            guarded(n < m, lambda m=m, c=c: rise(m, c, True).wait_send())
+            guarded(n > m, lambda m=m, c=c: rise(m, c, False).wait_send())
     for copy in sent:
         copy.wait_send()
 
@@ -341,16 +407,18 @@
             pltpu.VMEM((N, height, slice_w), bf16),
             pltpu.VMEM((N, height, slice_w), bf16),
             pltpu.VMEM((N, height, slice_w), bf16),
+            pltpu.VMEM((N, height, slice_w), bf16),
             pltpu.VMEM((blocks, up_weight.shape[0], BW), bf16),
             pltpu.VMEM((blocks, down_weight.shape[0], BW), bf16),
             pltpu.VMEM(pred_in.shape, bf16),
-            dma((N, nc)), dma((N, nc)),
+            dma((N, nc, 2)), dma((N, nc)),
             dma((N,)), dma((N,)),
             dma((N, nc)), dma((N, nc)),
             dma((N,)), dma((N,)),
             dma((N,)), dma((N,)),
             dma((N,)), dma((N,)),
             dma((N,)), dma((N,)),
+            dma((N, nc)), dma((N, nc)),
             dma((N, nc)), dma((N, nc)),
             dma((N, nc)), dma((N, nc)),
             dma((3, blocks)),

time: 134 us -> 117 us (0.87)
  the two profiles are of different devices: /device:TPU:25 before, /device:TPU:0 now
where the time goes in v2:
time: 117 us
  Pallas kernels  107 us (91%)
  local copies, waits for them, and re-layouts  5.02 us (4%)
  other arithmetic  2.61 us (2%)
  between operations  2.03 us (2%)
    pallas_call x1, Pallas kernels, fused_device(): pl.pallas_call(layer_kernel, out_shape=jax.ShapeDtypeStruct(features.shap...  107 us
    unnamed x4, local copies, waits for them, and re-layouts  2.68 us

profile of v2, /device:TPU:0, one launch (start us, length us, event | category | flops | bytes accessed | tf_op | source)
XLA Modules:
  0.0 117.1 jit_solution(8118510927376863456)
XLA Ops:
  0.0 0.7 iota_compare_fusion.1
  0.7 0.8 and_reduce_fusion
  1.5 0.2 select_reduce_fusion.1
  1.7 0.6 dynamic_slice.12
  2.9 0.7 dynamic_slice.13
  4.9 0.1 pad_add_fusion
  5.0 0.2 dynamic-slice_reduce_fusion
  5.2 0.1 and_convert_fusion.pick_ref
  5.3 0.1 copy.14
  5.4 0.1 reshape.147.ids
  5.5 0.7 bitcast_convert_fusion
  6.2 0.1 multiply_reduce_fusion
  6.2 0.7 reshape.151.gain_ref
  6.9 0.9 copy.15
  7.8 0.0 copy-start
  7.8 1.0 copy-done
  8.9 107.5 %shard_map.91 = bf16[112,2304]{1,0:T(8,128)(2,1)S(1)} custom-call(s32[8]{0:T(128)S(1)} %reshape.147.ids, bf16[112,2304]{1,0:T(8,128)(2,1)S(1)} %copy-done, f32[1,2304]{1,0:T(1,128)S(1)} %reshape.151.gain_ref, f32[2,1,128]{2,1,0:T(1,128)S(1)} %bitcast.8, f32[2,1,128]{2,1,0:T(1,128)S(1)} %and_convert_fusion.pick_ref, bf16[256,128]{1,0:T(8,128)(2,1)S(1)} %pad.4.pout_ref, ...), custom_call_target="tpu_custom_call" | custom-call | tf_op jit(solution)/shard_map/pallas_call | solution.py:392
  116.3 0.8 copy.17
  (6 shorter events, 0.0 us)
Async XLA Ops:
  7.8 1.0 copy-start

commit v3 on v2

--- a/solution.py
+++ b/solution.py
@@ -86,9 +86,9 @@
 
 
 def layer_kernel(
-    ids, x_ref, gain_ref, bias_ref, pick_ref, pout_ref, up_hbm, down_hbm, pin_hbm, out_ref,
+    active, counts, x_ref, gain_in, bias_in, pout_in, up_hbm, down_hbm, pin_hbm, out_ref,
     zbuf, zgain, xin, stats, terms, term_out, pre_out, pre_in, hid, outp, pbuf, rup, rdn,
-    up_v, down_v, pin_v,
+    up_v, down_v, pin_v, gain_ref, bias_v, pick_v, pout_v, total_v, square_v,
     z_ss, z_rs, g_ss, g_rs, x_ss, x_rs, s_ss, s_rs, t_ss, t_rs, p_ss, p_rs, h_ss, h_rs,
     o_ss, o_rs, u_ss, u_rs, d_ss, d_rs, w_sem,
 ):
@@ -119,9 +119,6 @@
                 for j in range(blocks)
             ]
         )
-    for group in loads:
-        for load in group:
-            load.start()
     zpeer = [lax.rem(n + k, N) for k in range(N)]
 
     def plane(k):
@@ -135,6 +132,7 @@
         pl.semaphore_signal(barrier, inc=1, device_id=pdev(ppeer[k]), device_id_type=MESH)
     pl.semaphore_wait(barrier, 2 * (N - 1))
 
+    gain_ref[...] = gain_in[...].astype(f32)
     sent = []
 
     def go(copy):
@@ -158,8 +156,21 @@
         guarded(n > 0, lambda c=c: hop(n, c, False, x_ref.at[rows(c)]).start())
     for k in range(1, N):
         go(send(gain_ref, zgain.at[n], g_ss.at[k], g_rs.at[n], zdev(zpeer[k])))
+    for group in loads:
+        for load in group:
+            load.start()
     zbuf[n] = x_ref[...]
     zgain[n] = gain_ref[...]
+    values = x_ref[...].astype(f32)
+    total_v[...] = jnp.sum(values, axis=1, keepdims=True)
+    square_v[...] = jnp.sum(values * values, axis=1, keepdims=True)
+    place = lax.broadcasted_iota(jnp.int32, (1, 128), 1)
+    for j in range(blocks):
+        bias_v[j] = bias_in[:, j * BW : (j + 1) * BW].astype(f32)
+        pick_v[j] = jnp.where(place == n * blocks + j, 1.0, 0.0).astype(f32)
+    pick_v[blocks] = jnp.zeros((1, 128), f32)
+    pout_v[...] = jnp.zeros(pout_v.shape, bf16)
+    pout_v[:, : pout_in.shape[1]] = pout_in[...]
 
     def inward(m, c, src):
         return send(src, xin.at[g, rows(c)], x_ss.at[m, c], x_rs.at[g, c], pdev(m))
@@ -176,22 +187,16 @@
                     send(x_ref.at[rows(c)], block, z_ss.at[m, c, 0], z_rs.at[m, c], zdev(zpeer[1])).wait_recv()
                     guarded(n < N - 1 if up else n > 0, lambda: hop(m, c, up, block).start())
                     guarded(m != g, lambda: inward(m, c, block).start())
+                    v = zbuf[m, rows(c)].astype(f32)
+                    total_v[rows(c)] += jnp.sum(v, axis=1, keepdims=True)
+                    square_v[rows(c)] += jnp.sum(v * v, axis=1, keepdims=True)
 
                 guarded(m >= 0 if up else m < N, arrive)
     for k in range(1, N):
         m = zpeer[k]
         send(gain_ref, zgain.at[m], g_ss.at[1], g_rs.at[m], zdev(m)).wait_recv()
 
-    def add_stats(m, carry):
-        total, square = carry
-        v = zbuf[m].astype(f32)
-        return (
-            total + jnp.sum(v, axis=1, keepdims=True),
-            square + jnp.sum(v * v, axis=1, keepdims=True),
-        )
-
-    zero = jnp.zeros((x_ref.shape[0], 1), f32)
-    total, square = lax.fori_loop(0, N, add_stats, (zero, zero))
+    total, square = total_v[...], square_v[...]
     mean = total / full
     scale = lax.rsqrt(square / full - mean * mean + epsilon)
     lane = lax.broadcasted_iota(jnp.int32, (x_ref.shape[0], 128), 1)
@@ -210,13 +215,22 @@
         return acc + jnp.dot(norm(zbuf[m], mean, scale, zgain[m]), block, preferred_element_type=f32)
 
     factor = lax.fori_loop(0, N, add_factor, jnp.zeros((x_ref.shape[0], pin_v.shape[1]), f32))
-    term_out[...] = jnp.dot(factor.astype(bf16), pout_ref[...], preferred_element_type=f32).astype(bf16)
+    term_out[...] = jnp.dot(factor.astype(bf16), pout_v[...], preferred_element_type=f32).astype(bf16)
     terms[n] = term_out[...]
     for k in range(1, N):
         go(send(term_out, terms.at[n], t_ss.at[k], t_rs.at[n], zdev(zpeer[k])))
 
+    def chosen(q):
+        low, high = jnp.int32(blocks), jnp.int32(-1)
+        for k in range(active.shape[1]):
+            local = active[q, k] - n * blocks
+            inside = (k < counts[q]) & (local >= 0) & (local < blocks)
+            low = jnp.minimum(low, jnp.where(inside, local, blocks))
+            high = jnp.maximum(high, jnp.where(inside, local, -1))
+        return low, jnp.where(high > low, high, blocks)
+
     def picked(ref, q):
-        return jnp.concatenate((ref[ids[2 * q]], ref[ids[2 * q + 1]]), axis=1)
+        return jnp.concatenate([ref[jnp.minimum(i, blocks - 1)] for i in chosen(q)], axis=1)
 
     for load in loads[1]:
         load.wait()
@@ -253,14 +267,16 @@
     for m in range(N):
         scores = scores + terms[m].astype(f32)
     gates = jax.nn.sigmoid(scores)
-    gate = [jnp.sum(gates * pick_ref[j], axis=1, keepdims=True) for j in range(CAP)]
+    mine = chosen(g)
+    gate = [jnp.sum(gates * pick_v[i], axis=1, keepdims=True) for i in mine]
+    bias = [bias_v[jnp.minimum(i, blocks - 1)] for i in mine]
     pre = pre_out[g].astype(f32)
     for k in range(1, N):
         q = ppeer[k]
         send(pre_out.at[g], pre_in.at[q], p_ss.at[1], p_rs.at[q], pdev(q)).wait_recv()
         pre = pre + pre_in[q].astype(f32)
     hidden = [
-        (jnp.maximum(pre[:, j * BW : (j + 1) * BW] + bias_ref[j], 0.0) * gate[j]).astype(bf16)
+        (jnp.maximum(pre[:, j * BW : (j + 1) * BW] + bias[j], 0.0) * gate[j]).astype(bf16)
         for j in range(2)
     ]
     hid[g] = jnp.concatenate(hidden, axis=1)
@@ -362,28 +378,8 @@
 def fused_device(
     features, ln_gain, up_weight, up_bias, down_weight, pred_in, pred_out, active, counts
 ):
-    neuron = lax.axis_index("neuron")
     blocks = up_weight.shape[1] // BW
     height, slice_w = features.shape
-    live = lax.broadcasted_iota(jnp.int32, active.shape, 1) < counts[:, None]
-    local_ids = neuron * blocks + jnp.arange(blocks, dtype=jnp.int32)
-    chosen = jnp.any((active[:, :, None] == local_ids[None, None, :]) & live[:, :, None], axis=1)
-    number = jnp.arange(blocks, dtype=jnp.int32)[None, :]
-    lowest = jnp.min(jnp.where(chosen, number, blocks), axis=1)
-    highest = jnp.max(jnp.where(chosen, number, -1), axis=1)
-    places = jnp.stack((jnp.minimum(lowest, blocks - 1), jnp.maximum(highest, 0)), axis=1)
-    group = lax.axis_index(("row", "sub"))
-    mine = lax.dynamic_index_in_dim(places, group, 0, keepdims=False)
-    low = lax.dynamic_index_in_dim(lowest, group, 0, keepdims=False)
-    high = lax.dynamic_index_in_dim(highest, group, 0, keepdims=False)
-    valid = jnp.stack((high >= 0, high > low))
-    lanes = jnp.arange(128, dtype=jnp.int32)[None, :]
-    pick = ((lanes == neuron * blocks + mine[:, None]) & valid[:, None]).astype(jnp.float32)[:, None]
-    hot = (number == mine[:, None]).astype(jnp.float32)
-    bias_table = up_bias.reshape(blocks, BW).astype(jnp.float32)
-    bias = jnp.sum(hot[:, :, None] * bias_table[None], axis=1)[:, None]
-    gain = ln_gain.astype(jnp.float32).reshape(1, slice_w)
-    pout = jnp.pad(pred_out, ((0, 0), (0, 128 - pred_out.shape[1])))
     vmem = pl.BlockSpec(memory_space=pltpu.VMEM)
     hbm = pl.BlockSpec(memory_space=pl.ANY)
     nc = len(PARTS)
@@ -392,7 +388,7 @@
     return pl.pallas_call(
         layer_kernel,
         out_shape=jax.ShapeDtypeStruct(features.shape, bf16),
-        in_specs=[pl.BlockSpec(memory_space=pltpu.SMEM)] + [vmem] * 5 + [hbm] * 3,
+        in_specs=[pl.BlockSpec(memory_space=pltpu.SMEM)] * 2 + [vmem] * 4 + [hbm] * 3,
         out_specs=vmem,
         scratch_shapes=[
             pltpu.VMEM((N, height, slice_w), bf16),
@@ -411,6 +407,12 @@
             pltpu.VMEM((blocks, up_weight.shape[0], BW), bf16),
             pltpu.VMEM((blocks, down_weight.shape[0], BW), bf16),
             pltpu.VMEM(pred_in.shape, bf16),
+            pltpu.VMEM((1, slice_w), f32),
+            pltpu.VMEM((blocks, 1, BW), f32),
+            pltpu.VMEM((blocks + 1, 1, 128), f32),
+            pltpu.VMEM((pred_out.shape[0], 128), bf16),
+            pltpu.VMEM((height, 1), f32),
+            pltpu.VMEM((height, 1), f32),
             dma((N, nc, 2)), dma((N, nc)),
             dma((N,)), dma((N,)),
             dma((N, nc)), dma((N, nc)),
@@ -426,7 +428,10 @@
         compiler_params=pltpu.CompilerParams(
             collective_id=0, has_side_effects=True, vmem_limit_bytes=50 * 1024 * 1024
         ),
-    )(places.reshape(-1), features, gain, bias, pick, pout, up_weight, down_weight, pred_in)
+    )(
+        active, counts, features, ln_gain.reshape(1, -1), up_bias.reshape(1, -1), pred_out,
+        up_weight, down_weight, pred_in,
+    )
 
 
 def solution(mesh):

time: 117 us -> 113 us (0.966)
  other arithmetic: 2.61 us -> 0 us
  between operations: 2.03 us -> 0.02 us
    dynamic_slice x3 -> x0, local copies, waits for them, and re-layouts: 1.45 us -> none  [the longest x1 0.67 us: fused_device(): low = lax.dynamic_index_in_dim(lowest, group, 0, keepdims=False)]
    unnamed x4 -> x8, local copies, waits for them, and re-layouts: 2.68 us -> 4.02 us
where the time goes in v3:
time: 113 us
  Pallas kernels  107 us (95%)
  local copies, waits for them, and re-layouts  5.41 us (5%)
    pallas_call x1, Pallas kernels, fused_device(): pl.pallas_call(layer_kernel, out_shape=jax.ShapeDtypeStruct(features.shap...  107 us
    unnamed x8, local copies, waits for them, and re-layouts  4.02 us

profile of v3, /device:TPU:0, one launch (start us, length us, event | category | flops | bytes accessed | tf_op | source)
XLA Modules:
  0.0 112.8 jit_solution(11796972735113852255)
XLA Ops:
  0.0 0.7 reshape.7.bias_in
  0.7 0.7 reshape.6.gain_in
  1.4 0.9 copy.10.pout_in
  2.2 0.0 copy-start
  2.3 1.0 copy-done
  3.3 0.0 copy-start.1
  3.3 0.7 copy-done.1
  4.0 0.0 copy-start.2
  4.0 0.7 copy-done.2
  4.6 107.4 %shard_map.91 = bf16[112,2304]{1,0:T(8,128)(2,1)S(1)} custom-call(s32[4,8]{1,0:T(4,128)S(1)} %copy-done.1, s32[4]{0:T(128)S(1)} %copy-done.2, bf16[112,2304]{1,0:T(8,128)(2,1)S(1)} %copy-done, bf16[1,2304]{1,0:T(2,128)(2,1)S(1)} %reshape.6.gain_in, bf16[1,1152]{1,0:T(2,128)(2,1)S(1)} %reshape.7.bias_in, bf16[256,36]{1,0:T(8,128)(2,1)S(1)} %copy.10.pout_in, ...), custom_call_target="tpu_custom_call" | custom-call | tf_op jit(solution)/shard_map/pallas_call | solution.py:388
  112.0 0.8 copy.12
Async XLA Ops:
  2.2 1.0 copy-start
  3.3 0.7 copy-start.1
  4.0 0.7 copy-start.2

commit v4 on v3

--- a/solution.py
+++ b/solution.py
@@ -82,6 +82,7 @@
 
 N = 4
 PARTS = ((0, 32), (32, 32), (64, 32), (96, 16))
+HALVES = ((0, 64, (0, 1)), (64, 48, (2, 3)))
 MESH = pl.DeviceIdType.MESH
 
 
@@ -177,8 +178,8 @@
 
     for c in chunks:
         guarded(n != g, lambda c=c: inward(n, c, x_ref.at[rows(c)]).start())
-    for far in range(1, N):
-        for c in chunks:
+    def arrivals(far, h):
+        for c in HALVES[h][2]:
             for up in (True, False):
                 m = n - far if up else n + far
 
@@ -192,33 +193,15 @@
                     square_v[rows(c)] += jnp.sum(v * v, axis=1, keepdims=True)
 
                 guarded(m >= 0 if up else m < N, arrive)
-    for k in range(1, N):
-        m = zpeer[k]
-        send(gain_ref, zgain.at[m], g_ss.at[1], g_rs.at[m], zdev(m)).wait_recv()
-
-    total, square = total_v[...], square_v[...]
-    mean = total / full
-    scale = lax.rsqrt(square / full - mean * mean + epsilon)
-    lane = lax.broadcasted_iota(jnp.int32, (x_ref.shape[0], 128), 1)
-    stats[g] = jnp.where(lane < 64, mean, scale)
-    for k in range(1, N):
-        go(send(stats.at[g], stats.at[g], s_ss.at[k], s_rs.at[g], pdev(ppeer[k])))
+    def wait_loads(i):
+        for load in loads[i]:
+            load.wait()
+
+    def half(h):
+        return pl.ds(HALVES[h][0], HALVES[h][1])
 
     def norm(values, mu, sc, gain):
         return ((values.astype(f32) - mu) * sc * gain).astype(bf16)
-
-    for load in loads[0]:
-        load.wait()
-
-    def add_factor(m, acc):
-        block = pin_v[pl.ds(pl.multiple_of(m * slice_w, 128), slice_w), :]
-        return acc + jnp.dot(norm(zbuf[m], mean, scale, zgain[m]), block, preferred_element_type=f32)
-
-    factor = lax.fori_loop(0, N, add_factor, jnp.zeros((x_ref.shape[0], pin_v.shape[1]), f32))
-    term_out[...] = jnp.dot(factor.astype(bf16), pout_v[...], preferred_element_type=f32).astype(bf16)
-    terms[n] = term_out[...]
-    for k in range(1, N):
-        go(send(term_out, terms.at[n], t_ss.at[k], t_rs.at[n], zdev(zpeer[k])))
 
     def chosen(q):
         low, high = jnp.int32(blocks), jnp.int32(-1)
@@ -232,84 +215,113 @@
     def picked(ref, q):
         return jnp.concatenate([ref[jnp.minimum(i, blocks - 1)] for i in chosen(q)], axis=1)
 
-    for load in loads[1]:
-        load.wait()
-    xin[g] = zbuf[g]
-
-    def up(k, _):
-        q = plane(k)
-
-        @pl.when(k < N)
-        def _():
-            for c in chunks:
-                send(x_ref.at[rows(c)], xin.at[q, rows(c)], x_ss.at[1, c], x_rs.at[q, c], pdev(q)).wait_recv()
-            send(stats.at[g], stats.at[q], s_ss.at[1], s_rs.at[q], pdev(q)).wait_recv()
-
-        st = stats[q]
-        normed = norm(xin[q], st[:, 0:1], st[:, 64:65], zgain[g])
-        pre = jnp.dot(normed, picked(up_v, q), preferred_element_type=f32)
-        pre_out[q] = pre.astype(bf16)
-
-        @pl.when(k < N)
-        def _():
-            send(pre_out.at[q], pre_in.at[g], p_ss.at[lax.rem(k, N)], p_rs.at[g], pdev(q)).start()
-
-        return 0
-
-    lax.fori_loop(1, N + 1, up, 0)
-    for k in range(1, N):
-        sent.append(send(pre_out.at[ppeer[k]], pre_in.at[g], p_ss.at[k], p_rs.at[g], pdev(ppeer[k])))
-
-    for k in range(1, N):
-        m = zpeer[k]
-        send(term_out, terms.at[m], t_ss.at[1], t_rs.at[m], zdev(m)).wait_recv()
-    scores = jnp.zeros((x_ref.shape[0], 128), f32)
-    for m in range(N):
-        scores = scores + terms[m].astype(f32)
-    gates = jax.nn.sigmoid(scores)
-    mine = chosen(g)
-    gate = [jnp.sum(gates * pick_v[i], axis=1, keepdims=True) for i in mine]
-    bias = [bias_v[jnp.minimum(i, blocks - 1)] for i in mine]
-    pre = pre_out[g].astype(f32)
-    for k in range(1, N):
-        q = ppeer[k]
-        send(pre_out.at[g], pre_in.at[q], p_ss.at[1], p_rs.at[q], pdev(q)).wait_recv()
-        pre = pre + pre_in[q].astype(f32)
-    hidden = [
-        (jnp.maximum(pre[:, j * BW : (j + 1) * BW] + bias[j], 0.0) * gate[j]).astype(bf16)
-        for j in range(2)
-    ]
-    hid[g] = jnp.concatenate(hidden, axis=1)
-    for k in range(1, N):
-        go(send(hid.at[g], hid.at[g], h_ss.at[k], h_rs.at[g], pdev(ppeer[k])))
-
-    for load in loads[2]:
-        load.wait()
-
-    def down(k, _):
-        q = plane(k)
-
-        @pl.when(k < N)
-        def _():
-            send(hid.at[g], hid.at[q], h_ss.at[1], h_rs.at[q], pdev(q)).wait_recv()
-
-        outp[q] = lax.dot_general(
-            hid[q], picked(down_v, q), (((1,), (1,)), ((), ())), preferred_element_type=f32
-        ).astype(bf16)
-        return 0
+    def stats_of(h):
+        at = half(h)
+        mean = total_v[at] / full
+        scale = lax.rsqrt(square_v[at] / full - mean * mean + epsilon)
+        lane = lax.broadcasted_iota(jnp.int32, (HALVES[h][1], 128), 1)
+        stats[g, at] = jnp.where(lane < 64, mean, scale)
+        xin[g, at] = zbuf[g, at]
+        for k in range(1, N):
+            go(send(stats.at[g, at], stats.at[g, at], s_ss.at[k, h], s_rs.at[g, h], pdev(ppeer[k])))
+
+    def factors(h):
+        at = half(h)
+        st = stats[g, at]
+
+        def add_factor(m, acc):
+            block = pin_v[pl.ds(pl.multiple_of(m * slice_w, 128), slice_w), :]
+            normed = norm(zbuf[m, at], st[:, 0:1], st[:, 64:65], zgain[m])
+            return acc + jnp.dot(normed, block, preferred_element_type=f32)
+
+        factor = lax.fori_loop(0, N, add_factor, jnp.zeros((HALVES[h][1], pin_v.shape[1]), f32))
+        term_out[at] = jnp.dot(factor.astype(bf16), pout_v[...], preferred_element_type=f32).astype(bf16)
+        terms[n, at] = term_out[at]
+        for k in range(1, N):
+            go(send(term_out.at[at], terms.at[n, at], t_ss.at[k, h], t_rs.at[n, h], zdev(zpeer[k])))
+
+    def pre_send(k, q, h):
+        at = half(h)
+        return send(pre_out.at[q, at], pre_in.at[g, at], p_ss.at[lax.rem(k, N), h], p_rs.at[g, h], pdev(q))
+
+    def ups(h):
+        at = half(h)
+
+        def up(k, _):
+            q = plane(k)
+
+            @pl.when(k < N)
+            def _():
+                for c in HALVES[h][2]:
+                    send(x_ref.at[rows(c)], xin.at[q, rows(c)], x_ss.at[1, c], x_rs.at[q, c], pdev(q)).wait_recv()
+                send(stats.at[g, at], stats.at[q, at], s_ss.at[1, h], s_rs.at[q, h], pdev(q)).wait_recv()
+
+            st = stats[q, at]
+            normed = norm(xin[q, at], st[:, 0:1], st[:, 64:65], zgain[g])
+            pre_out[q, at] = jnp.dot(normed, picked(up_v, q), preferred_element_type=f32).astype(bf16)
+
+            @pl.when(k < N)
+            def _():
+                pre_send(k, q, h).start()
+
+            return 0
+
+        lax.fori_loop(1, N + 1, up, 0)
+        for k in range(1, N):
+            sent.append(pre_send(jnp.int32(k), ppeer[k], h))
+
+    def hiddens(h):
+        at = half(h)
+        for k in range(1, N):
+            m = zpeer[k]
+            send(term_out.at[at], terms.at[m, at], t_ss.at[1, h], t_rs.at[m, h], zdev(m)).wait_recv()
+        scores = jnp.zeros((HALVES[h][1], 128), f32)
+        for m in range(N):
+            scores = scores + terms[m, at].astype(f32)
+        gates = jax.nn.sigmoid(scores)
+        mine = chosen(g)
+        gate = [jnp.sum(gates * pick_v[i], axis=1, keepdims=True) for i in mine]
+        bias = [bias_v[jnp.minimum(i, blocks - 1)] for i in mine]
+        pre = pre_out[g, at].astype(f32)
+        for k in range(1, N):
+            q = ppeer[k]
+            send(pre_out.at[g, at], pre_in.at[q, at], p_ss.at[1, h], p_rs.at[q, h], pdev(q)).wait_recv()
+            pre = pre + pre_in[q, at].astype(f32)
+        hidden = [
+            (jnp.maximum(pre[:, j * BW : (j + 1) * BW] + bias[j], 0.0) * gate[j]).astype(bf16)
+            for j in range(2)
+        ]
+        hid[g, at] = jnp.concatenate(hidden, axis=1)
+        for k in range(1, N):
+            go(send(hid.at[g, at], hid.at[g, at], h_ss.at[k, h], h_rs.at[g, h], pdev(ppeer[k])))
 
     def outward(k, c):
         q = ppeer[k]
         return send(outp.at[q, rows(c)], pbuf.at[g, rows(c)], o_ss.at[k, c], o_rs.at[g, c], pdev(q))
 
-    lax.fori_loop(1, 3, down, 0)
-    for c in chunks:
-        for k in (1, 2):
-            go(outward(k, c))
-    lax.fori_loop(3, N + 1, down, 0)
-    for c in chunks:
-        go(outward(3, c))
-    pbuf[g] = outp[g]
+    def downs(h):
+        at = half(h)
+
+        def down(k, _):
+            q = plane(k)
+
+            @pl.when(k < N)
+            def _():
+                send(hid.at[g, at], hid.at[q, at], h_ss.at[1, h], h_rs.at[q, h], pdev(q)).wait_recv()
+
+            outp[q, at] = lax.dot_general(
+                hid[q, at], picked(down_v, q), (((1,), (1,)), ((), ())), preferred_element_type=f32
+            ).astype(bf16)
+            return 0
+
+        lax.fori_loop(1, 3, down, 0)
+        for c in HALVES[h][2]:
+            for k in (1, 2):
+                go(outward(k, c))
+        lax.fori_loop(3, N + 1, down, 0)
+        for c in HALVES[h][2]:
+            go(outward(3, c))
+        pbuf[g, at] = outp[g, at]
 
     def rise(m, c, up):
         at = pbuf.at[m, rows(c)]
@@ -327,8 +339,8 @@
 
         guarded(m != g, wait)
 
-    for c in chunks:
-        for far in (3, 2, 1):
+    def rises(far, h):
+        for c in HALVES[h][2]:
             for up in (True, False):
                 m = n + far if up else n - far
 
@@ -346,6 +358,33 @@
                     rise(m, c, up).start()
 
                 guarded(m < N if up else m >= 0, forward)
+    for far in range(1, N):
+        arrivals(far, 0)
+    for k in range(1, N):
+        m = zpeer[k]
+        send(gain_ref, zgain.at[m], g_ss.at[1], g_rs.at[m], zdev(m)).wait_recv()
+
+    stats_of(0)
+    wait_loads(0)
+    arrivals(1, 1)
+    factors(0)
+    wait_loads(1)
+    ups(0)
+    arrivals(2, 1)
+    hiddens(0)
+    wait_loads(2)
+    arrivals(3, 1)
+    stats_of(1)
+    downs(0)
+    factors(1)
+    rises(3, 0)
+    ups(1)
+    rises(2, 0)
+    hiddens(1)
+    rises(1, 0)
+    downs(1)
+    for far in (3, 2, 1):
+        rises(far, 1)
     for c in chunks:
         own(n, c)
 
@@ -416,10 +455,10 @@
             dma((N, nc, 2)), dma((N, nc)),
             dma((N,)), dma((N,)),
             dma((N, nc)), dma((N, nc)),
-            dma((N,)), dma((N,)),
-            dma((N,)), dma((N,)),
-            dma((N,)), dma((N,)),
-            dma((N,)), dma((N,)),
+            dma((N, 2)), dma((N, 2)),
+            dma((N, 2)), dma((N, 2)),
+            dma((N, 2)), dma((N, 2)),
+            dma((N, 2)), dma((N, 2)),
             dma((N, nc)), dma((N, nc)),
             dma((N, nc)), dma((N, nc)),
             dma((N, nc)), dma((N, nc)),

time: 113 us -> 98.5 us (0.87)
  Pallas kernels: 107 us -> 92.7 us
    pallas_call x1, Pallas kernels: 107 us -> 92.7 us  [fused_device(): pl.pallas_call(layer_kernel, out_shape=jax.ShapeDtypeStruct(features.shap...]
where the time goes in v4:
time: 98.5 us; the launch traced here: 98.2 us
  Pallas kernels  92.7 us (94%)
  local copies, waits for them, and re-layouts  5.41 us (5%)
    pallas_call x1, Pallas kernels, fused_device(): pl.pallas_call(layer_kernel, out_shape=jax.ShapeDtypeStruct(features.shap...  92.7 us
    unnamed x8, local copies, waits for them, and re-layouts  4.02 us

profile of v4, /device:TPU:0, one launch (start us, length us, event | category | flops | bytes accessed | tf_op | source)
XLA Modules:
  0.0 98.2 jit_solution(4897270811330327722)
XLA Ops:
  0.0 0.7 reshape.7.bias_in
  0.7 0.7 reshape.6.gain_in
  1.4 0.9 copy.10.pout_in
  2.2 0.0 copy-start
  2.3 1.0 %copy-done = bf16[112,2304]{1,0:T(8,128)(2,1)S(1)} copy-done((bf16[112,2304]{1,0:T(8,128)(2,1)S(1)}, bf16[112,2304]{1,0:T(8,128)(2,1)}, u32[]{:S(2)}) %copy-start) | copy-done | bytes 516120
  3.3 0.0 copy-start.1
  3.3 0.7 copy-done.1
  4.0 0.0 copy-start.2
  4.0 0.7 copy-done.2
  4.6 92.7 %shard_map.91 = bf16[112,2304]{1,0:T(8,128)(2,1)S(1)} custom-call(s32[4,8]{1,0:T(4,128)S(1)} %copy-done.1, s32[4]{0:T(128)S(1)} %copy-done.2, bf16[112,2304]{1,0:T(8,128)(2,1)S(1)} %copy-done, bf16[1,2304]{1,0:T(2,128)(2,1)S(1)} %reshape.6.gain_in, bf16[1,1152]{1,0:T(2,128)(2,1)S(1)} %reshape.7.bias_in, bf16[256,36]{1,0:T(8,128)(2,1)S(1)} %copy.10.pout_in, ...), custom_call_target="tpu_custom_call" | custom-call | tf_op jit(solution)/shard_map/pallas_call | solution.py:427
  97.4 0.8 copy.12
Async XLA Ops:
  2.2 1.0 %copy-start = (bf16[112,2304]{1,0:T(8,128)(2,1)S(1)}, bf16[112,2304]{1,0:T(8,128)(2,1)}, u32[]{:S(2)}) copy-start(bf16[112,2304]{1,0:T(8,128)(2,1)} %x_ref.1) | copy-start | bytes 1548292
  3.3 0.7 copy-start.1
  4.0 0.7 copy-start.2

commit v5 on v4

--- a/solution.py
+++ b/solution.py
@@ -87,9 +87,9 @@
 
 
 def layer_kernel(
-    active, counts, x_ref, gain_in, bias_in, pout_in, up_hbm, down_hbm, pin_hbm, out_ref,
+    active, counts, x_ref, vectors, pout_hbm, up_hbm, down_hbm, pin_hbm, out_ref,
     zbuf, zgain, xin, stats, terms, term_out, pre_out, pre_in, hid, outp, pbuf, rup, rdn,
-    up_v, down_v, pin_v, gain_ref, bias_v, pick_v, pout_v, total_v, square_v,
+    up_v, down_v, pin_v, gain_ref, bias_v, pick_v, pout_in, pout_v, total_v, square_v,
     z_ss, z_rs, g_ss, g_rs, x_ss, x_rs, s_ss, s_rs, t_ss, t_rs, p_ss, p_rs, h_ss, h_rs,
     o_ss, o_rs, u_ss, u_rs, d_ss, d_rs, w_sem,
 ):
@@ -112,7 +112,12 @@
         )
 
     blocks = up_v.shape[0]
-    loads = [[pltpu.make_async_copy(pin_hbm, pin_v, w_sem.at[0, 0])]]
+    loads = [
+        [
+            pltpu.make_async_copy(pin_hbm, pin_v, w_sem.at[0, 0]),
+            pltpu.make_async_copy(pout_hbm, pout_in, w_sem.at[0, 1]),
+        ]
+    ]
     for i, (a, b) in enumerate(((up_hbm, up_v), (down_hbm, down_v))):
         loads.append(
             [
@@ -133,7 +138,7 @@
         pl.semaphore_signal(barrier, inc=1, device_id=pdev(ppeer[k]), device_id_type=MESH)
     pl.semaphore_wait(barrier, 2 * (N - 1))
 
-    gain_ref[...] = gain_in[...].astype(f32)
+    gain_ref[...] = vectors[:, :slice_w].astype(f32)
     sent = []
 
     def go(copy):
@@ -167,11 +172,9 @@
     square_v[...] = jnp.sum(values * values, axis=1, keepdims=True)
     place = lax.broadcasted_iota(jnp.int32, (1, 128), 1)
     for j in range(blocks):
-        bias_v[j] = bias_in[:, j * BW : (j + 1) * BW].astype(f32)
+        bias_v[j] = vectors[:, slice_w + j * BW : slice_w + (j + 1) * BW].astype(f32)
         pick_v[j] = jnp.where(place == n * blocks + j, 1.0, 0.0).astype(f32)
     pick_v[blocks] = jnp.zeros((1, 128), f32)
-    pout_v[...] = jnp.zeros(pout_v.shape, bf16)
-    pout_v[:, : pout_in.shape[1]] = pout_in[...]
 
     def inward(m, c, src):
         return send(src, xin.at[g, rows(c)], x_ss.at[m, c], x_rs.at[g, c], pdev(m))
@@ -366,6 +369,8 @@
 
     stats_of(0)
     wait_loads(0)
+    pout_v[...] = jnp.zeros(pout_v.shape, bf16)
+    pout_v[:, : pout_in.shape[1]] = pout_in[...]
     arrivals(1, 1)
     factors(0)
     wait_loads(1)
@@ -427,7 +432,7 @@
     return pl.pallas_call(
         layer_kernel,
         out_shape=jax.ShapeDtypeStruct(features.shape, bf16),
-        in_specs=[pl.BlockSpec(memory_space=pltpu.SMEM)] * 2 + [vmem] * 4 + [hbm] * 3,
+        in_specs=[pl.BlockSpec(memory_space=pltpu.SMEM)] * 2 + [vmem] * 2 + [hbm] * 4,
         out_specs=vmem,
         scratch_shapes=[
             pltpu.VMEM((N, height, slice_w), bf16),
@@ -449,6 +454,7 @@
             pltpu.VMEM((1, slice_w), f32),
             pltpu.VMEM((blocks, 1, BW), f32),
             pltpu.VMEM((blocks + 1, 1, 128), f32),
+            pltpu.VMEM(pred_out.shape, bf16),
             pltpu.VMEM((pred_out.shape[0], 128), bf16),
             pltpu.VMEM((height, 1), f32),
             pltpu.VMEM((height, 1), f32),
@@ -468,7 +474,7 @@
             collective_id=0, has_side_effects=True, vmem_limit_bytes=50 * 1024 * 1024
         ),
     )(
-        active, counts, features, ln_gain.reshape(1, -1), up_bias.reshape(1, -1), pred_out,
+        active, counts, features, jnp.concatenate((ln_gain, up_bias)).reshape(1, -1), pred_out,
         up_weight, down_weight, pred_in,
     )
 

time: 98.5 us -> 97.8 us (level)
  local copies, waits for them, and re-layouts: 5.41 us -> 4.03 us
    reshape x2 -> x1, local copies, waits for them, and re-layouts: 1.39 us -> 0.01 us  [fused_device(): jnp.concatenate((ln_gain, up_bias)).reshape(1, -1)]
where the time goes in v5:
time: 97.8 us; the launch traced here: 97.5 us
  Pallas kernels  92.7 us (95%)
  local copies, waits for them, and re-layouts  4.03 us (4%)
    pallas_call x1, Pallas kernels, fused_device(): pl.pallas_call(layer_kernel, out_shape=jax.ShapeDtypeStruct(features.shap...  92.7 us
    unnamed x8, local copies, waits for them, and re-layouts  4.02 us

profile of v5, /device:TPU:0, one launch (start us, length us, event | category | flops | bytes accessed | tf_op | source)
XLA Modules:
  0.0 97.5 jit_solution(13347061438127822521)
XLA Ops:
  0.0 0.7 pad_maximum_fusion
  0.7 0.9 copy.10.pout_hbm
  1.6 0.0 copy-start
  1.6 1.0 %copy-done = bf16[112,2304]{1,0:T(8,128)(2,1)S(1)} copy-done((bf16[112,2304]{1,0:T(8,128)(2,1)S(1)}, bf16[112,2304]{1,0:T(8,128)(2,1)}, u32[]{:S(2)}) %copy-start) | copy-done | bytes 516120
  2.6 0.0 copy-start.1
  2.6 0.7 copy-done.1
  3.3 0.0 copy-start.2
  3.3 0.7 copy-done.2
  4.0 92.7 %shard_map.91 = bf16[112,2304]{1,0:T(8,128)(2,1)S(1)} custom-call(s32[4,8]{1,0:T(4,128)S(1)} %copy-done.1, s32[4]{0:T(128)S(1)} %copy-done.2, bf16[112,2304]{1,0:T(8,128)(2,1)S(1)} %copy-done, bf16[1,3456]{1,0:T(2,128)(2,1)S(1)} %reshape.3.vectors, bf16[256,36]{1,0:T(8,128)(2,1)S(1)} %copy.10.pout_hbm, bf16[2304,1152]{1,0:T(8,128)(2,1)} %up_hbm.1, ...), custom_call_target="tpu_custom_call" | custom-call | tf_op jit(solution)/shard_map/pallas_call | solution.py:432
  96.7 0.8 copy.12
  (1 shorter events, 0.0 us)
Async XLA Ops:
  1.6 1.0 %copy-start = (bf16[112,2304]{1,0:T(8,128)(2,1)S(1)}, bf16[112,2304]{1,0:T(8,128)(2,1)}, u32[]{:S(2)}) copy-start(bf16[112,2304]{1,0:T(8,128)(2,1)} %x_ref.1) | copy-start | bytes 1548292
  2.6 0.7 copy-start.1
  3.3 0.7 copy-start.2
